TPU v7x, 32 devices: a whole 2x2x4 slice. The times are simulated.
32 devices in a mesh: cache: 8 (over z, y), cand: 4 (over x, core).
Axes of the slice: x: 2, y: 2, z: 4, core: 2. Of those that a mesh axis runs over, the one named last changes fastest.
Arguments:
- cand_states: bfloat16 [1024, 16, 1024], P('cand', 'cache'), may hold values from -6 to 6
- in_proj: bfloat16 [1024, 4, 1024], P(None, None, 'cand'), may hold values from -0.1875 to 0.1875
- out_proj: bfloat16 [1024, 1024], P('cand'), may hold values from -0.1875 to 0.1875
- history: bfloat16 [8, 16, 2, 512, 1024], P('cache', None, None, None, 'cand'), may hold values from -6 to 6
- lengths: int32 [16], replicated, may hold values from 2048 to 4096, as said below
- rank_users: int32 [16], replicated, may hold values from 0 to 15, each once
- recency_bias: float32 [8, 14], P('cand'), may hold values from -4 to 4
- score_weight: float32 [1024], replicated, may hold values from -0.1875 to 0.1875
Outputs:
- layer_out: bfloat16 [1024, 16, 1024], P('cand', 'cache')
- scores: float32 [1024, 16], P('cand', 'cache')
Inputs may be any that keep to these rules, and one draw needn't show every extreme that they name: `lengths`: every length is a multiple of 128; some user's length is exactly 4096. `rank_users`: each user is ranked in exactly one slot.
All inputs are finite; a program needn't handle non-finite values.
Results may differ from a plain program's by a relative error of at most 0.008.
Values may be sent and summed in bfloat16 or wider, within the bound.
No kernel may reach another device: no remote copies, remote signals or barrier semaphores. Data moves between devices by JAX's collectives and lax.ppermute only.
A program may use at most 128 MiB of HBM per device.

v0:
```python
import math

import jax
import jax.numpy as jnp
from jax import lax
from jax.sharding import PartitionSpec as P

BLOCK = 128


EPSILON = 1e-06


def bucket_index(distance, bucket_count):
    powers = 2 ** jnp.arange(bucket_count - 1, dtype=jnp.int32)
    return jnp.sum((distance[..., None] >= powers).astype(jnp.int32), axis=-1)


def local(cand_states, in_proj, out_proj, history, lengths, rank_users, recency_bias, score_weight):
    cache_count = lax.axis_size("cache")
    my_group = lax.axis_index("cache")
    cand_rows, users_here, width = cand_states.shape
    head_width = in_proj.shape[2]
    heads_here, bucket_count = recency_bias.shape
    head_size = head_width // heads_here
    scale = head_size ** (-0.5)
    float_states = cand_states.astype(jnp.float32)
    normed = (
        float_states
        * lax.rsqrt(jnp.mean(float_states * float_states, axis=-1, keepdims=True) + EPSILON)
    ).astype(jnp.bfloat16)
    proj_matrix = in_proj.reshape(width, 4 * head_width)
    shard_rows = lax.all_gather(normed, "cand", axis=0, tiled=True)
    row_count = shard_rows.shape[0]
    product = jnp.dot(
        shard_rows.reshape(row_count * users_here, width),
        proj_matrix,
        preferred_element_type=jnp.float32,
    )
    projected = (
        jax.nn.silu(product).astype(jnp.bfloat16).reshape(row_count, users_here, 4, head_width)
    )
    all_cands = projected.shape[0]
    stored = history[0]
    page_events = stored.shape[2]
    chosen = jnp.take(stored, rank_users, axis=0).reshape(
        cache_count, users_here, 2, page_events, head_width
    )
    arrived = lax.all_to_all(chosen, "cache", split_axis=0, concat_axis=0, tiled=True)
    total_events = cache_count * page_events
    key_block = min(1024, total_events)
    group = math.gcd(cache_count, max(1, key_block // BLOCK))
    groups = cache_count // group
    block_rows = group * BLOCK
    span = cache_count * BLOCK
    my_users = lax.dynamic_slice_in_dim(rank_users, my_group * users_here, users_here)
    my_lengths = jnp.take(lengths, my_users)
    local_rows = jnp.arange(block_rows, dtype=jnp.int32)
    bucket_ids = jnp.arange(bucket_count, dtype=jnp.int32)
    bias_columns = recency_bias.T

    def attend_user(member, gated):
        user = my_users[member]
        length = my_lengths[member]
        own = lax.dynamic_index_in_dim(projected, member, 1, keepdims=False)
        gates = own[:, 0].reshape(all_cands, heads_here, head_size)
        own_values = own[:, 1].reshape(all_cands, heads_here, head_size)
        queries = own[:, 2].reshape(all_cands, heads_here, head_size)
        own_keys = own[:, 3].reshape(all_cands, heads_here, head_size)

        def add_block(step, totals):
            page_block = step // groups
            first_shard = step % groups * group
            piece = lax.dynamic_slice(
                arrived,
                (first_shard, member, 0, page_block * BLOCK, 0),
                (group, 1, 2, BLOCK, head_width),
            )
            block_keys = piece[:, 0, 0].reshape(block_rows, heads_here, head_size)
            block_values = piece[:, 0, 1].reshape(block_rows, heads_here, head_size)
            shard_of_row = first_shard + local_rows // BLOCK
            positions = (
                page_block * cache_count + jnp.remainder(shard_of_row - user, cache_count)
            ) * BLOCK + local_rows % BLOCK
            usable = positions < length
            distance = jnp.maximum(length - positions, 0)
            onehot = (bucket_index(distance, bucket_count)[:, None] == bucket_ids[None, :]).astype(
                jnp.float32
            )
            block_bias = jnp.dot(onehot, bias_columns, precision=lax.Precision.HIGHEST)
            scores = (
                jnp.einsum("chd,khd->chk", queries, block_keys, preferred_element_type=jnp.float32)
                * scale
                + block_bias.T[None]
            )
            weights = jnp.where(usable[None, None, :], jax.nn.silu(scores), 0.0).astype(
                jnp.bfloat16
            )
            return totals + jnp.einsum(
                "chk,khd->chd", weights, block_values, preferred_element_type=jnp.float32
            )

        used_steps = (length + span - 1) // span * groups
        totals = lax.fori_loop(
            0, used_steps, add_block, jnp.zeros((all_cands, heads_here, head_size), jnp.float32)
        )
        self_scores = (
            jnp.sum(queries.astype(jnp.float32) * own_keys.astype(jnp.float32), axis=-1) * scale
            + recency_bias[:, 0][None, :]
        )
        totals = totals + jax.nn.silu(self_scores)[..., None] * own_values.astype(jnp.float32)
        normalized = totals * lax.rsqrt(jnp.mean(totals * totals, axis=-1, keepdims=True) + EPSILON)
        result = (
            (normalized * gates.astype(jnp.float32))
            .astype(jnp.bfloat16)
            .reshape(all_cands, 1, head_width)
        )
        return lax.dynamic_update_slice_in_dim(gated, result, member, 1)

    gated = lax.fori_loop(
        0, users_here, attend_user, jnp.zeros((all_cands, users_here, head_width), jnp.bfloat16)
    )
    spread = lax.all_to_all(gated, "cand", split_axis=0, concat_axis=2, tiled=True)
    full_out = lax.all_gather(out_proj, "cand", axis=0, tiled=True)
    branch_sum = jnp.dot(
        spread.reshape(cand_rows * users_here, width), full_out, preferred_element_type=jnp.float32
    ).reshape(cand_rows, users_here, width)
    layer_sum = float_states + branch_sum
    scores_out = jnp.sum(layer_sum * score_weight, axis=-1)
    return (layer_sum.astype(jnp.bfloat16), scores_out)


def solution(mesh):
    in_specs = (
        P("cand", "cache", None),
        P(None, None, "cand"),
        P("cand", None),
        P("cache", None, None, None, "cand"),
        P(),
        P(),
        P("cand", None),
        P(),
    )
    out_specs = (P("cand", "cache", None), P("cand", "cache"))
    return jax.shard_map(local, mesh=mesh, in_specs=in_specs, out_specs=out_specs, check_vma=False)
```

profile of v0, /device:TPU:0, one launch (start us, length us, event | category | flops | bytes accessed | tf_op | source)
XLA Modules:
  0.0 370.7 jit_solution(9034929239054916214)
XLA Ops:
  8.6 8.1 %gather_fusion.1 = bf16[16,2,512,256]{3,2,1,0:T(8,128)(2,1)} fusion(bf16[16,2,512,256]{3,2,1,0:T(8,128)(2,1)} %bitcast.121, s32[1024]{0:T(1024)S(1)} %pad_clamp_fusion), kind=kCustom, calls=%fused_computation.1 | custom fusion | bytes 16777280 | tf_op jit(solution)/shard_map/jit(_take)/gather | solution.py:46
  16.8 7.5 %broadcast_select_fusion = bf16[8,2,2,512,256]{4,3,2,1,0:T(8,128)(2,1)} fusion(bf16[8,2,2,512,256]{4,3,2,1,0:T(8,128)(2,1)} %bitcast.120, pred[8,2]{1,0:T(8,128)(4,1)S(1)} %broadcast_in_dim.60), kind=kLoop, calls=%fused_computation.92 | loop fusion | flops 4194304 | bytes 16777232 | tf_op jit(solution)/shard_map/jit(_take)/select_n | solution.py:46
  24.2 7.4 %all-to-all-start = ((bf16[8,2,2,512,256]{4,3,2,1,0:T(8,128)(2,1)}), bf16[8,2,2,512,256]{4,3,2,1,0:T(8,128)(2,1)}, u32[]{:S(2)}, u32[]{:S(2)}) async-start(bf16[8,2,2,512,256]{4,3,2,1,0:T(8,128)(2,1)} %broadcast_select_fusion), calls=%async_computation | async-start | bytes 16777216 | tf_op jit(solution)/shard_map/all_to_all | solution.py:49
  34.1 1.8 copy.52
  36.8 33.2 %all-gather.3.cloned.1.call-done = bf16[1024,2,1024]{2,0,1:T(8,128)(2,1)} async-done(((bf16[256,2,1024]{2,0,1:T(8,128)(2,1)}), bf16[1024,2,1024]{2,0,1:T(8,128)(2,1)}) %all-gather.3.cloned.1.call-update) | async-done | bytes 4194320 | tf_op jit(solution)/shard_map/all_gather | solution.py:33
  70.0 8.5 %copy.42 = bf16[1024,2,1024]{2,1,0:T(2,128)(2,1)} copy(bf16[1024,2,1024]{2,0,1:T(8,128)(2,1)} %all-gather.3.cloned.1.call-done) | data formatting | bytes 8388608 | tf_op jit(solution)/shard_map/all_gather | solution.py:33
  78.4 7.3 %reshape.287 = bf16[2048,1024]{1,0:T(8,128)(2,1)} reshape(bf16[1024,2,1024]{2,1,0:T(2,128)(2,1)} %copy.42) | data formatting | bytes 8388608 | tf_op jit(solution)/shard_map/reshape | solution.py:36
  85.8 9.5 %multiply_convert_fusion = bf16[2048,1024]{1,0:T(8,128)(2,1)} fusion(bf16[2048,1024]{1,0:T(8,128)(2,1)} %reshape.287, bf16[1024,1024]{1,0:T(8,128)(2,1)S(1)} %bitcast.127), kind=kOutput, calls=%fused_computation.91 | convolution fusion | flops 4305453056 | bytes 10485760 | tf_op jit(solution)/shard_map/dot_general | solution.py:35
  95.3 7.8 %reshape.289 = bf16[1024,2,4,256]{3,2,1,0:T(4,128)(2,1)} reshape(bf16[2048,1024]{1,0:T(8,128)(2,1)} %multiply_convert_fusion) | data formatting | bytes 8388608 | tf_op jit(solution)/shard_map/reshape | solution.py:41
  103.1 111.7 %all-to-all-done = bf16[8,2,2,512,256]{4,3,2,1,0:T(8,128)(2,1)} async-done(((bf16[8,2,2,512,256]{4,3,2,1,0:T(8,128)(2,1)}), bf16[8,2,2,512,256]{4,3,2,1,0:T(8,128)(2,1)}, u32[]{:S(2)}, u32[]{:S(2)}) %all-to-all-start) | async-done | bytes 8388640 | tf_op jit(solution)/shard_map/all_to_all | solution.py:49
  214.8 14.7 %copy.44 = bf16[8,2,2,512,256]{3,0,4,2,1:T(8,128)(2,1)} copy(bf16[8,2,2,512,256]{4,3,2,1,0:T(8,128)(2,1)} %all-to-all-done) | data formatting | bytes 16777216
  229.5 107.4 %while.69 = (s32[]{:T(128)}, bf16[1024,2,256]{0,2,1:T(8,128)(2,1)}, s32[2]{0:T(128)S(1)}, s32[2]{0:T(128)S(1)}, bf16[1024,2,4,256]{3,2,1,0:T(4,128)(2,1)}, /*ind...) while((s32[]{:T(128)}, bf16[1024,2,256]{0,2,1:T(8,128)(2,1)}, ...), condition=%wide.region_7.8_spmd.clone.clone, body=%wide.region_1.7_spmd.clone.clone.sunk | while | flops 1095469440 | bytes 39492888 | solution.py:120
  230.7 3.6 constant_dynamic-slice_fusion.5
  234.4 3.0 copy.60
  240.3 38.6 %while.70 = (s32[]{:T(128)}, f32[1024,2,128]{0,2,1:T(8,128)S(1)}, s32[]{:T(128)}, bf16[8,2,2,512,256]{3,0,4,2,1:T(8,128)(2,1)}, s32[]{:T(128)}, /*index=5*/s32[1...) while((s32[]{:T(128)}, f32[1024,2,128]{0,2,1:T(8,128)S(1)}, ...), condition=%wide.region_4.4_spmd.clone, body=%wide.region_2.3_spmd.clone.sunk | while | flops 1091257728 | bytes 7936575 | solution.py:104
  240.4 1.3 constant_dynamic-slice_fusion.6
  244.0 1.3 fusion.93
  245.3 4.7 %fusion.94 = f32[1024,2,128]{0,2,1:T(8,128)S(1)} fusion(f32[1024,2,128]{0,2,1:T(8,128)S(1)} %get-tuple-element.1374, bf16[1024,2,128]{0,2,1:T(8,128)(2,1)S(1)} %squeeze.138, f32[2,1024]{1,0:T(2,128)S(1)} %convolution_bitcast_fusion.2, pred[1024]{0:T(1024)(128)(4,1)S(1)} %fusion.93, bf16[1024,2,128]{0,2,1:T(8,128)(2,1)S(1)} %squeeze.139, ...), kind=kOutput, calls=%fused_computation.19.clone.1 | convolution fusion | flops 1090781184 | bytes 3679232 | tf_op jit(solution)/shard_map/while/body/eval_jaxpr/while/body/chk,khd->chd/dot_general | solution.py:99
  250.0 1.3 constant_dynamic-slice_fusion.6
  253.7 1.3 fusion.93
  255.0 4.7 %fusion.94 = f32[1024,2,128]{0,2,1:T(8,128)S(1)} fusion(f32[1024,2,128]{0,2,1:T(8,128)S(1)} %get-tuple-element.1374, bf16[1024,2,128]{0,2,1:T(8,128)(2,1)S(1)} %squeeze.138, f32[2,1024]{1,0:T(2,128)S(1)} %convolution_bitcast_fusion.2, pred[1024]{0:T(1024)(128)(4,1)S(1)} %fusion.93, bf16[1024,2,128]{0,2,1:T(8,128)(2,1)S(1)} %squeeze.139, ...), kind=kOutput, calls=%fused_computation.19.clone.1 | convolution fusion | flops 1090781184 | bytes 3679232 | tf_op jit(solution)/shard_map/while/body/eval_jaxpr/while/body/chk,khd->chd/dot_general | solution.py:99
  259.7 1.3 constant_dynamic-slice_fusion.6
  263.3 1.3 fusion.93
  264.6 4.7 %fusion.94 = f32[1024,2,128]{0,2,1:T(8,128)S(1)} fusion(f32[1024,2,128]{0,2,1:T(8,128)S(1)} %get-tuple-element.1374, bf16[1024,2,128]{0,2,1:T(8,128)(2,1)S(1)} %squeeze.138, f32[2,1024]{1,0:T(2,128)S(1)} %convolution_bitcast_fusion.2, pred[1024]{0:T(1024)(128)(4,1)S(1)} %fusion.93, bf16[1024,2,128]{0,2,1:T(8,128)(2,1)S(1)} %squeeze.139, ...), kind=kOutput, calls=%fused_computation.19.clone.1 | convolution fusion | flops 1090781184 | bytes 3679232 | tf_op jit(solution)/shard_map/while/body/eval_jaxpr/while/body/chk,khd->chd/dot_general | solution.py:99
  269.3 1.3 constant_dynamic-slice_fusion.6
  273.0 1.3 fusion.93
  274.3 4.7 %fusion.94 = f32[1024,2,128]{0,2,1:T(8,128)S(1)} fusion(f32[1024,2,128]{0,2,1:T(8,128)S(1)} %get-tuple-element.1374, bf16[1024,2,128]{0,2,1:T(8,128)(2,1)S(1)} %squeeze.138, f32[2,1024]{1,0:T(2,128)S(1)} %convolution_bitcast_fusion.2, pred[1024]{0:T(1024)(128)(4,1)S(1)} %fusion.93, bf16[1024,2,128]{0,2,1:T(8,128)(2,1)S(1)} %squeeze.139, ...), kind=kOutput, calls=%fused_computation.19.clone.1 | convolution fusion | flops 1090781184 | bytes 3679232 | tf_op jit(solution)/shard_map/while/body/eval_jaxpr/while/body/chk,khd->chd/dot_general | solution.py:99
  279.0 1.5 fusion.84
  280.8 1.3 fusion.85
  284.4 3.6 constant_dynamic-slice_fusion.5
  288.1 3.0 copy.60
  294.0 38.6 %while.70 = (s32[]{:T(128)}, f32[1024,2,128]{0,2,1:T(8,128)S(1)}, s32[]{:T(128)}, bf16[8,2,2,512,256]{3,0,4,2,1:T(8,128)(2,1)}, s32[]{:T(128)}, /*index=5*/s32[1...) while((s32[]{:T(128)}, f32[1024,2,128]{0,2,1:T(8,128)S(1)}, ...), condition=%wide.region_4.4_spmd.clone, body=%wide.region_2.3_spmd.clone.sunk | while | flops 1091257728 | bytes 7936575 | solution.py:104
  294.1 1.3 constant_dynamic-slice_fusion.6
  297.7 1.3 fusion.93
  299.0 4.7 %fusion.94 = f32[1024,2,128]{0,2,1:T(8,128)S(1)} fusion(f32[1024,2,128]{0,2,1:T(8,128)S(1)} %get-tuple-element.1374, bf16[1024,2,128]{0,2,1:T(8,128)(2,1)S(1)} %squeeze.138, f32[2,1024]{1,0:T(2,128)S(1)} %convolution_bitcast_fusion.2, pred[1024]{0:T(1024)(128)(4,1)S(1)} %fusion.93, bf16[1024,2,128]{0,2,1:T(8,128)(2,1)S(1)} %squeeze.139, ...), kind=kOutput, calls=%fused_computation.19.clone.1 | convolution fusion | flops 1090781184 | bytes 3679232 | tf_op jit(solution)/shard_map/while/body/eval_jaxpr/while/body/chk,khd->chd/dot_general | solution.py:99
  303.7 1.3 constant_dynamic-slice_fusion.6
  308.7 4.7 %fusion.94 = f32[1024,2,128]{0,2,1:T(8,128)S(1)} fusion(f32[1024,2,128]{0,2,1:T(8,128)S(1)} %get-tuple-element.1374, bf16[1024,2,128]{0,2,1:T(8,128)(2,1)S(1)} %squeeze.138, f32[2,1024]{1,0:T(2,128)S(1)} %convolution_bitcast_fusion.2, pred[1024]{0:T(1024)(128)(4,1)S(1)} %fusion.93, bf16[1024,2,128]{0,2,1:T(8,128)(2,1)S(1)} %squeeze.139, ...), kind=kOutput, calls=%fused_computation.19.clone.1 | convolution fusion | flops 1090781184 | bytes 3679232 | tf_op jit(solution)/shard_map/while/body/eval_jaxpr/while/body/chk,khd->chd/dot_general | solution.py:99
  313.4 1.3 constant_dynamic-slice_fusion.6
  317.0 1.3 fusion.93
  318.3 4.7 %fusion.94 = f32[1024,2,128]{0,2,1:T(8,128)S(1)} fusion(f32[1024,2,128]{0,2,1:T(8,128)S(1)} %get-tuple-element.1374, bf16[1024,2,128]{0,2,1:T(8,128)(2,1)S(1)} %squeeze.138, f32[2,1024]{1,0:T(2,128)S(1)} %convolution_bitcast_fusion.2, pred[1024]{0:T(1024)(128)(4,1)S(1)} %fusion.93, bf16[1024,2,128]{0,2,1:T(8,128)(2,1)S(1)} %squeeze.139, ...), kind=kOutput, calls=%fused_computation.19.clone.1 | convolution fusion | flops 1090781184 | bytes 3679232 | tf_op jit(solution)/shard_map/while/body/eval_jaxpr/while/body/chk,khd->chd/dot_general | solution.py:99
  323.0 1.3 constant_dynamic-slice_fusion.6
  328.0 4.7 %fusion.94 = f32[1024,2,128]{0,2,1:T(8,128)S(1)} fusion(f32[1024,2,128]{0,2,1:T(8,128)S(1)} %get-tuple-element.1374, bf16[1024,2,128]{0,2,1:T(8,128)(2,1)S(1)} %squeeze.138, f32[2,1024]{1,0:T(2,128)S(1)} %convolution_bitcast_fusion.2, pred[1024]{0:T(1024)(128)(4,1)S(1)} %fusion.93, bf16[1024,2,128]{0,2,1:T(8,128)(2,1)S(1)} %squeeze.139, ...), kind=kOutput, calls=%fused_computation.19.clone.1 | convolution fusion | flops 1090781184 | bytes 3679232 | tf_op jit(solution)/shard_map/while/body/eval_jaxpr/while/body/chk,khd->chd/dot_general | solution.py:99
  332.7 1.5 fusion.84
  334.5 1.3 fusion.85
  336.9 2.6 copy.46
  339.5 17.0 %all_to_all.20 = bf16[1024,2,256]{2,1,0:T(2,128)(2,1)S(1)} all-to-all(bf16[1024,2,256]{2,1,0:T(2,128)(2,1)S(1)} %copy.46), channel_id=1, replica_groups=mesh['cache'=8,'cand'=4] {'cand'}, dimensions={0} | all-to-all | bytes 2097152 | tf_op jit(solution)/shard_map/all_to_all | solution.py:123
  358.1 3.7 %multiply_reduce_fusion.1 = (f32[256,2]{0,1:T(2,128)}, bf16[256,2,1024]{2,0,1:T(8,128)(2,1)S(1)}) fusion(f32[1024]{0:T(1024)S(1)} %copy-done.11, bf16[256,2,1024]{2,0,1:T(8,128)(2,1)S(1)} %dot_general.27, bf16[1024,1024]{1,0:T(8,128)(2,1)} %all-gather.5.cloned.1.call-done, bf16[256,2,1024]{2,1,0:T(2,128)(2,1)S(1)} %copy-done.4), kind=kOutput, calls=%fused_computation.100 | convolution fusion | flops 1076362752 | bytes 5249024 | tf_op jit(solution)/shard_map/dot_general | solution.py:125
  361.9 2.0 copy.48
  (146 shorter events, 37.2 us)
Async XLA Ops:
  7.2 29.0 %copy-start = (s32[16]{0:T(128)S(1)}, s32[16]{0:T(128)}, u32[]{:S(2)}) copy-start(s32[16]{0:T(128)} %param.16) | copy-start | bytes 196
  24.2 7.5 %copy-start.3 = (bf16[256,2,1024]{2,1,0:T(2,128)(2,1)S(1)}, bf16[256,2,1024]{2,1,0:T(2,128)(2,1)}, u32[]{:S(2)}) copy-start(bf16[256,2,1024]{2,1,0:T(2,128)(2,1)} %param.12) | copy-start | bytes 3145732
  24.2 190.6 %all-to-all-start = ((bf16[8,2,2,512,256]{4,3,2,1,0:T(8,128)(2,1)}), bf16[8,2,2,512,256]{4,3,2,1,0:T(8,128)(2,1)}, u32[]{:S(2)}, u32[]{:S(2)}) async-start(bf16[8,2,2,512,256]{4,3,2,1,0:T(8,128)(2,1)} %broadcast_select_fusion), calls=%async_computation | async-start | bytes 16777216 | tf_op jit(solution)/shard_map/all_to_all | solution.py:49
  31.7 2.5 copy-start.5
  31.7 38.3 %all-gather.3.cloned.1.call-start = ((), (), s32[]{:S(2)}) async-start(), calls=%async_computation.2 | async-start | bytes 5242880 | tf_op jit(solution)/shard_map/all_gather | solution.py:33
  32.1 3.9 %copy-start.9 = (f32[2,14]{1,0:T(2,128)S(1)}, f32[2,14]{1,0:T(2,128)}, u32[]{:S(2)}) copy-start(f32[2,14]{1,0:T(2,128)} %param.18) | copy-start | bytes 340
  32.1 4.0 %copy-start.10 = (s32[16]{0:T(128)S(1)}, s32[16]{0:T(128)}, u32[]{:S(2)}) copy-start(s32[16]{0:T(128)} %param.17) | copy-start | bytes 196
  33.4 324.7 %all-gather.5.cloned.1.call-start = ((), (), s32[]{:S(2)}) async-start(), calls=%async_computation.3 | async-start | bytes 2621440 | tf_op jit(solution)/shard_map/all_gather | solution.py:124
  78.4 7.3 %copy-start.6 = (bf16[128,8,4,256]{3,1,2,0:T(8,128)(2,1)S(1)}, bf16[128,8,4,256]{3,1,2,0:T(8,128)(2,1)}, u32[]{:S(2)}) copy-start(bf16[128,8,4,256]{3,1,2,0:T(8,128)(2,1)} %copy.52) | copy-start | bytes 6291460
  238.5 1.8 copy-start.2
  279.0 3.2 copy-start.7
  282.2 1.0 copy-start.8
  292.2 1.8 copy-start.2
  332.7 3.2 copy-start.7
  335.9 1.0 copy-start.8
  336.9 21.3 %copy-start.4 = (bf16[256,2,1024]{2,1,0:T(2,128)(2,1)S(1)}, bf16[256,2,1024]{2,1,0:T(2,128)(2,1)}, u32[]{:S(2)}) copy-start(bf16[256,2,1024]{2,1,0:T(2,128)(2,1)} %param.12) | copy-start | bytes 3145732
  336.9 21.3 %copy-start.11 = (f32[1024]{0:T(1024)S(1)}, f32[1024]{0:T(1024)}, u32[]{:S(2)}) copy-start(f32[1024]{0:T(1024)} %param.19) | copy-start | bytes 12292
  357.3 6.6 %copy-start.1 = (s32[16]{0:T(128)S(1)}, s32[16]{0:T(128)}, u32[]{:S(2)}) copy-start(s32[16]{0:T(128)} %param.16) | copy-start | bytes 196
Sparse Core Ops, SparseCore 0:
  34.1 35.8 all-gather.2
  71.5 22.5 all-gather.4
where the time goes:
time: 373 us; the launch traced here: 371 us
  waiting for transfers between devices  146 us (39%)
  local copies, waits for them, and re-layouts  91.6 us (25%)
  matrix products  54.3 us (15%)
  other arithmetic  38.5 us (10%)
  blocking collectives  17 us (5%)
  between operations  14.2 us (4%)
  starting transfers between devices  7.5 us (2%)
    all_to_all x1, waiting for transfers between devices, local(): lax.all_to_all(chosen, 'cache', split_axis=0, concat_axis=0, tiled=True)  112 us
    dot_general x8, matrix products, add_block(): jnp.einsum('chk,khd->chd', weights, block_values, preferred_element_type=...  37.5 us
    all_gather x1, waiting for transfers between devices, local(): shard_rows = lax.all_gather(normed, 'cand', axis=0, tiled=True)  33.2 us
    unnamed x22, local copies, waits for them, and re-layouts  18.7 us
    all_to_all x1, blocking collectives, local(): lax.all_to_all(gated, 'cand', split_axis=0, concat_axis=2, tiled=True)  17 us
    dynamic_slice x4, local copies, waits for them, and re-layouts, attend_user(): own = lax.dynamic_index_in_dim(projected, member, 1, keepdims=False)  13.2 us
    slice x8, local copies, waits for them, and re-layouts, add_block(): block_keys = piece[:, 0, 0].reshape(block_rows, heads_here, head_size)  10.4 us
    lt x8, other arithmetic, add_block(): usable = positions < length  10.3 us
  transfers between devices with their start and end apart: 3, of which 2 were waited for; matrix products, arithmetic and copies ran while one was open for 43% of the time, Pallas kernels for 0%

commit v1 on v0

v1 whole, which is shorter than its diff:
```python
import functools

import jax
import jax.numpy as jnp
from jax import lax
from jax.experimental import pallas as pl
from jax.experimental.pallas import tpu as pltpu
from jax.sharding import PartitionSpec as P

BLOCK = 128
EPSILON = 1e-06
MASKED = -1e30
VMEM = 48 * 1024 * 1024


def params():
    return pltpu.CompilerParams(vmem_limit_bytes=VMEM)


def tied(*arrays):
    return lax.optimization_barrier(arrays)


def bias_rows(recency_bias, most_blocks):
    bucket_count = recency_bias.shape[1]
    ends = jnp.arange(1, most_blocks + 1, dtype=jnp.int32)[:, None] * BLOCK
    distance = ends - jnp.arange(BLOCK, dtype=jnp.int32)[None, :]
    bucket = sum((distance >= 2**k).astype(jnp.int32) for k in range(bucket_count - 1))
    rows = sum(
        jnp.where(bucket[None] == b, recency_bias[:, b][:, None, None], 0.0)
        for b in range(bucket_count)
    )
    past = jnp.full((recency_bias.shape[0], 1, BLOCK), MASKED, jnp.float32)
    return jnp.concatenate([past, rows * 0.5], axis=1)


def attend_kernel(cache_count, heads, pick, queries, own, other, table, out):
    rows, width = queries.shape
    size = width // heads
    events = own.shape[3]
    chunk = min(2 * BLOCK, events)
    blocks_used = pick[1]
    for head in range(heads):
        columns = slice(head * size, (head + 1) * size)
        query = queries[:, columns]
        total = jnp.zeros((rows, size), jnp.float32)
        for place, page in ((2, own), (3, other)):
            shift = pick[place]
            for first in range(0, events, chunk):
                bias = []
                for block in range(first // BLOCK, (first + chunk) // BLOCK):
                    left = jnp.maximum(blocks_used - (block * cache_count + shift), 0)
                    bias.append(table[head, pl.ds(left, 1), :])
                bias = jnp.concatenate(bias, axis=1)
                keys = page[0, 0, 0, first : first + chunk, columns]
                values = page[0, 0, 1, first : first + chunk, columns]
                half = (
                    lax.dot_general(
                        query, keys, (((1,), (1,)), ((), ())), preferred_element_type=jnp.float32
                    )
                    + bias
                )
                weights = (half + half * jnp.tanh(half)).astype(jnp.bfloat16)
                total = total + jnp.dot(weights, values, preferred_element_type=jnp.float32)
        out[:, columns] = total.astype(jnp.bfloat16)


def attend(cache_count, pick, queries, own, other, table):
    rows, width = queries.shape
    heads = table.shape[0]
    events = own.shape[3]
    tile = min(256, rows)
    return pl.pallas_call(
        functools.partial(attend_kernel, cache_count, heads),
        grid_spec=pltpu.PrefetchScalarGridSpec(
            num_scalar_prefetch=1,
            grid=(rows // tile,),
            in_specs=[
                pl.BlockSpec((tile, width), lambda i, s: (i, 0)),
                pl.BlockSpec((1, 1, 2, events, width), lambda i, s: (0, s[0], 0, 0, 0)),
                pl.BlockSpec((1, 1, 2, events, width), lambda i, s: (0, 0, 0, 0, 0)),
                pl.BlockSpec(table.shape, lambda i, s: (0, 0, 0)),
            ],
            out_specs=pl.BlockSpec((tile, width), lambda i, s: (i, 0)),
        ),
        out_shape=jax.ShapeDtypeStruct((rows, width), jnp.bfloat16),
        compiler_params=params(),
        cost_estimate=pl.CostEstimate(
            flops=8 * rows * width * events,
            bytes_accessed=4 * rows * width + 8 * events * width,
            transcendentals=2 * rows * heads * events,
        ),
        name="attend",
    )(pick, queries, own, other, table)


def project_kernel(scales, count, *refs):
    blocks, weight, outs = refs[:count], refs[count], refs[count + 1 :]
    rows = blocks[0].shape[0]
    width = outs[0].shape[1]
    for i, block in enumerate(blocks):
        normed = block[...]
        for kind, (scale, out) in enumerate(zip(scales, outs)):
            product = jnp.dot(
                normed,
                weight[:, kind * width : (kind + 1) * width],
                preferred_element_type=jnp.float32,
            )
            half = product * 0.5
            out[i * rows : (i + 1) * rows, :] = (
                (half + half * jnp.tanh(half)) * scale
            ).astype(jnp.bfloat16)


def project(scales, blocks, weight):
    rows, depth = blocks[0].shape
    width = weight.shape[1] // len(scales)
    total = rows * len(blocks)
    shape = jax.ShapeDtypeStruct((total, width), jnp.bfloat16)
    return pl.pallas_call(
        functools.partial(project_kernel, scales, len(blocks)),
        out_shape=[shape] * len(scales),
        compiler_params=params(),
        cost_estimate=pl.CostEstimate(
            flops=2 * total * depth * weight.shape[1],
            bytes_accessed=2 * total * depth + 2 * depth * weight.shape[1],
            transcendentals=total * weight.shape[1],
        ),
        name="project",
    )(*blocks, weight)


def finish_kernel(count, first_bias, *refs):
    parts, (gates, values, queries, keys, out) = refs[:count], refs[count:]
    heads = first_bias.shape[0]
    size = gates.shape[1] // heads
    for head in range(heads):
        columns = slice(head * size, (head + 1) * size)
        total = sum(part[:, columns].astype(jnp.float32) for part in parts)
        half = (
            jnp.sum(
                queries[:, columns].astype(jnp.float32) * keys[:, columns].astype(jnp.float32),
                axis=-1,
                keepdims=True,
            )
            + first_bias[head] * 0.5
        )
        total = total + (half + half * jnp.tanh(half)) * values[:, columns].astype(jnp.float32)
        scale = lax.rsqrt(jnp.mean(total * total, axis=-1, keepdims=True) + EPSILON)
        out[:, columns] = (total * scale * gates[:, columns].astype(jnp.float32)).astype(
            jnp.bfloat16
        )


def finish(first_bias, parts, gates, values, queries, keys):
    rows, width = gates.shape
    tile = min(256, rows)
    spec = pl.BlockSpec((tile, width), lambda i: (i, 0))
    return pl.pallas_call(
        functools.partial(finish_kernel, len(parts)),
        grid=(rows // tile,),
        in_specs=[pl.BlockSpec(memory_space=pltpu.SMEM)] + [spec] * (len(parts) + 4),
        out_specs=spec,
        out_shape=jax.ShapeDtypeStruct((rows, width), jnp.bfloat16),
        compiler_params=params(),
        name="finish",
    )(first_bias, *parts, gates, values, queries, keys)


def combine_kernel(count, states, score_weight, *refs):
    gated, weights, (layer, scores) = refs[:count], refs[count : 2 * count], refs[2 * count :]
    total = states[...].astype(jnp.float32)
    for part, weight in zip(gated, weights):
        total = total + jnp.dot(part[...], weight[...], preferred_element_type=jnp.float32)
    layer[...] = total.astype(jnp.bfloat16)
    scores[...] = jnp.sum(total * score_weight[...], axis=-1, keepdims=True)


def combine(states, score_weight, gated, weights):
    rows, width = states.shape
    return pl.pallas_call(
        functools.partial(combine_kernel, len(gated)),
        out_shape=[
            jax.ShapeDtypeStruct((rows, width), jnp.bfloat16),
            jax.ShapeDtypeStruct((rows, 1), jnp.float32),
        ],
        compiler_params=params(),
        name="combine",
    )(states, score_weight[None], *gated, *weights)


def swap(axis, bit):
    return functools.partial(
        lax.ppermute, axis_name=axis, perm=[(i, i ^ bit) for i in range(lax.axis_size(axis))]
    )


def local(
    cand_states, in_proj, out_proj, history, lengths, rank_users, recency_bias, score_weight
):
    cache_count = lax.axis_size("cache")
    place = lax.axis_index("cache")
    cand_rows, users_here, width = cand_states.shape
    head_width = in_proj.shape[2]
    heads = recency_bias.shape[0]
    events = history.shape[3]
    half_scale = 0.5 * (head_width // heads) ** (-0.5)

    swap_core, swap_chip = swap("cand", 1), swap("cand", 2)
    swap_both = swap("cand", 3)
    swap_page = swap("cache", 1)

    states = jnp.moveaxis(cand_states, 1, 0)
    floats = states.astype(jnp.float32)
    normed = (
        floats * lax.rsqrt(jnp.mean(floats * floats, axis=-1, keepdims=True) + EPSILON)
    ).astype(jnp.bfloat16)
    in_matrix = in_proj.reshape(width, 4 * head_width)
    query_weight = in_matrix[:, 2 * head_width : 3 * head_width]
    table = bias_rows(recency_bias, cache_count * events // BLOCK)
    first_bias = recency_bias[:, 0]

    def slot_user(index, member):
        return lax.dynamic_index_in_dim(rank_users, index * users_here + member, 0, False)

    def page_of(user):
        return lax.dynamic_slice_in_dim(history, user, 1, 1)

    def pick_of(user, first, second):
        used = lax.dynamic_index_in_dim(lengths, user, 0, False) // BLOCK
        return jnp.stack(
            [user, used, jnp.remainder(first - user, cache_count), jnp.remainder(second - user, cache_count)]
        ).astype(jnp.int32)

    def gather_rows(member):
        mine = normed[member]
        across = swap_chip(mine)
        near = swap_core(mine)
        return [mine, near, across, swap_core(across)]

    def spread(gated):
        pieces = gated.reshape(4, cand_rows, head_width)
        return [pieces[0], swap_core(pieces[1]), swap_chip(pieces[2]), swap_both(pieces[3])]

    weight_rows = None

    if cache_count == 8 and users_here == 2:
        line = place // 2
        lane = place % 2
        at_end = (line == 0) | (line == 3)
        exchange_outer = swap("cache", 2)
        exchange_inner = functools.partial(
            lax.ppermute, axis_name="cache", perm=[(2, 4), (4, 2), (3, 5), (5, 3)]
        )
        visits = jnp.array(
            [
                [0, 1, 2, 3, 3, 2, 1, 0],
                [1, 2, 3, 0, 3, 2, 0, 1],
                [2, 1, 0, 3, 0, 1, 3, 2],
                [3, 2, 1, 0, 0, 1, 2, 3],
            ],
            jnp.int32,
        )
        visited = lax.dynamic_index_in_dim(visits, line, 0, False)
        members = (0, 0, 0, 0, 1, 1, 1, 1)
        picks, sent = [], []
        for step in range(8):
            user = slot_user(visited[step] * 2 + lane, members[step])
            picks.append(pick_of(user, place, place ^ 1))
            sent.append(slot_user(visited[step] * 2 + 1 - lane, members[step]))

        def partial_totals(step, queries, page):
            return attend(cache_count, picks[step], queries, history, page, table)

        def either(first, second):
            return jnp.where(at_end, first, second)

        pages = [swap_page(page_of(sent[0]))]
        rows_a = gather_rows(0)
        (query_a,) = project((half_scale,), rows_a, query_weight)
        page_next, query_a, rows_a[0] = tied(page_of(sent[1]), query_a, rows_a[0])
        pages.append(swap_page(page_next))
        rows_b = gather_rows(1)
        others_weight = jnp.concatenate(
            [in_matrix[:, : 2 * head_width], in_matrix[:, 3 * head_width :]], axis=1
        )

        outer, inner, totals = [], [], []
        to_outer, to_inner, queries = query_a, query_a, query_a
        for step in range(8):
            outer.append(exchange_outer(to_outer))
            inner.append(exchange_inner(to_inner))
            if step + 2 < 8:
                pages.append(swap_page(page_of(sent[step + 2])))
            totals.append(partial_totals(step, queries, pages[step]))
            if step == 0:
                (query_b,) = project((half_scale,), rows_b, query_weight)
                query_b, out_mine = tied(query_b, out_proj)
            if step == 1:
                rows_a = list(tied(*rows_a))
                gates_a, values_a, keys_a = project((1.0, 1.0, 1.0), rows_a, others_weight)
                out_across = swap_chip(out_mine)
            if step == 2:
                rows_b = list(tied(*rows_b))
                gates_b, values_b, keys_b = project((1.0, 1.0, 1.0), rows_b, others_weight)
                weight_rows = [out_mine, swap_core(out_mine), out_across, swap_core(out_across)]
            if step == 7:
                break
            outer[step], inner[step], totals[step], pages[-1] = tied(
                outer[step], inner[step], totals[step], pages[-1]
            )
            if step == 0:
                to_outer, to_inner = either(query_b, inner[0]), outer[0]
                queries = either(outer[0], inner[0])
            if step == 1:
                to_outer, to_inner = either(totals[1], inner[1]), outer[1]
                queries = either(outer[1], inner[1])
            if step == 2:
                to_outer, to_inner = either(totals[2], inner[2]), query_b
                queries = either(outer[2], outer[0])
            if step == 3:
                to_outer, to_inner = either(totals[3], inner[3]), outer[3] + totals[1]
                queries = either(outer[3], inner[2])
            if step == 4:
                to_outer, to_inner = either(totals[4], query_b), outer[4] + totals[2]
                queries = either(outer[4], inner[3])
            if step == 5:
                to_outer, to_inner = either(totals[5], inner[5] + totals[3]), outer[5] + totals[4]
                queries = either(outer[5], outer[1])
            if step == 6:
                to_outer, to_inner = either(totals[6], inner[6] + totals[6]), outer[6] + totals[5]
                queries = query_b
                zero = jnp.zeros_like(totals[0])
                gated_a = finish(
                    first_bias,
                    [totals[0], either(outer[6], outer[2]), inner[4]],
                    gates_a, values_a, query_a, keys_a,
                )
                spread_a = spread(gated_a)
        layer_a, scores_a = combine(states[0], score_weight, spread_a, weight_rows)
        gated_b = finish(
            first_bias, [totals[7], outer[7], inner[7]], gates_b, values_b, query_b, keys_b
        )
        layer_b, scores_b = combine(states[1], score_weight, spread(gated_b), weight_rows)
        return (
            jnp.stack([layer_a, layer_b], axis=1),
            jnp.concatenate([scores_a, scores_b], axis=1),
        )

    chosen = jnp.take(history[0], rank_users, axis=0).reshape(
        cache_count, users_here, 2, events, head_width
    )
    arrived = lax.all_to_all(chosen, "cache", split_axis=0, concat_axis=0, tiled=True)
    out_across = swap_chip(out_proj)
    weight_rows = [out_proj, swap_core(out_proj), out_across, swap_core(out_across)]
    layers, scores = [], []
    for member in range(users_here):
        user = slot_user(place, member)
        gates, values, queries, keys = project(
            (1.0, 1.0, half_scale, 1.0), gather_rows(member), in_matrix
        )

        def add_pair(step, total, user=user, member=member, queries=queries):
            pair = lax.dynamic_slice(
                arrived, (2 * step, member, 0, 0, 0), (2, 1, 2, events, head_width)
            )
            pick = pick_of(user, 2 * step, 2 * step + 1).at[0].set(0)
            part = attend(cache_count, pick, queries, pair[:1], pair[1:], table)
            return total + part.astype(jnp.float32)

        total = lax.fori_loop(
            0, cache_count // 2, add_pair, jnp.zeros(queries.shape, jnp.float32)
        )
        gated = finish(first_bias, [total], gates, values, queries, keys)
        layer, score = combine(states[member], score_weight, spread(gated), weight_rows)
        layers.append(layer)
        scores.append(score)
    return jnp.stack(layers, axis=1), jnp.concatenate(scores, axis=1)


def solution(mesh):
    in_specs = (
        P("cand", "cache", None),
        P(None, None, "cand"),
        P("cand", None),
        P("cache", None, None, None, "cand"),
        P(),
        P(),
        P("cand", None),
        P(),
    )
    out_specs = (P("cand", "cache", None), P("cand", "cache"))
    return jax.shard_map(local, mesh=mesh, in_specs=in_specs, out_specs=out_specs, check_vma=False)
```

time: 373 us -> 249 us (0.67)
  waiting for transfers between devices: 146 us -> 6.73 us
  local copies, waits for them, and re-layouts: 91.6 us -> 24.4 us
  Pallas kernels: 0 us -> 65.8 us
  between operations: 14.2 us -> 68.7 us
  matrix products: 54.3 us -> 0 us
  starting transfers between devices: 7.5 us -> 50.8 us
  blocking collectives: 17 us -> 0 us
  other arithmetic: 38.5 us -> 29.9 us
    all_to_all x1 -> x0, waiting for transfers between devices: 112 us -> none  [local(): lax.all_to_all(chosen, 'cache', split_axis=0, concat_axis=0, tiled=True)]
    pallas_call x0 -> x16, Pallas kernels: none -> 65.8 us  [the longest x8 49.4 us: attend(): pl.pallas_call(functools.partial(attend_kernel, cache_count, heads), grid...]
    dot_general x18 -> x0, matrix products: 54.3 us -> none  [the longest x8 37.5 us: add_block(): jnp.einsum('chk,khd->chd', weights, block_values, preferred_element_type=...]
    ppermute x0 -> x39, starting transfers between devices: none -> 50.8 us  [the longest x8 21.1 us: local(): outer.append(exchange_outer(to_outer))]
    all_gather x2 -> x0, waiting for transfers between devices: 33.2 us -> none  [the longest x1 33.2 us: local(): shard_rows = lax.all_gather(normed, 'cand', axis=0, tiled=True)]
    all_to_all x1 -> x0, blocking collectives: 17 us -> none  [local(): lax.all_to_all(gated, 'cand', split_axis=0, concat_axis=2, tiled=True)]
    reshape x2 -> x0, local copies, waits for them, and re-layouts: 15.2 us -> none  [the longest x1 7.82 us: local(): jax.nn.silu(product).astype(jnp.bfloat16)]
    select_n x12, other arithmetic: 8.32 us -> 18.9 us  [either(): return jnp.where(at_end, first, second)]
  transfers between devices with their start and end apart: 3 -> 39, of which waited for: 2 -> 5; matrix products, arithmetic and copies ran while one was open for 43% -> 15% of each run, Pallas kernels for 0% -> 26%
where the time goes in v1:
time: 249 us; the launch traced here: 246 us
  between operations  68.7 us (28%)
  Pallas kernels  65.8 us (26%)
  starting transfers between devices  50.8 us (20%)
  other arithmetic  29.9 us (12%)
  local copies, waits for them, and re-layouts  24.4 us (10%)
  waiting for transfers between devices  6.73 us (3%)
    pallas_call x8, Pallas kernels, attend(): pl.pallas_call(functools.partial(attend_kernel, cache_count, heads), grid...  49.4 us
    ppermute x8, starting transfers between devices, local(): outer.append(exchange_outer(to_outer))  21.1 us
    select_n x12, other arithmetic, either(): return jnp.where(at_end, first, second)  18.9 us
    unnamed x67, local copies, waits for them, and re-layouts  14.5 us
    ppermute x8, starting transfers between devices, local(): inner.append(exchange_inner(to_inner))  11.1 us
    pallas_call x4, Pallas kernels, project(): pl.pallas_call(functools.partial(project_kernel, scales, len(blocks)), ou...  8.38 us
    ppermute x6, starting transfers between devices, local(): pages.append(swap_page(page_of(sent[step + 2])))  6.85 us
    another operation x8, other arithmetic, pick_of(): jnp.stack([user, used, jnp.remainder(first - user, cache_count), jnp.rema...  5.71 us
  transfers between devices with their start and end apart: 39, of which 5 were waited for; matrix products, arithmetic and copies ran while one was open for 15% of the time, Pallas kernels for 26%

profile of v1, /device:TPU:0, one launch (start us, length us, event | category | flops | bytes accessed | tf_op | source)
XLA Modules:
  0.0 246.4 jit_solution(16183885546206841984)
XLA Ops:
  0.6 1.6 fusion
  2.2 1.5 fusion.1
  3.8 3.0 %collective-permute-start.1 = (bf16[256,1024]{1,0:T(8,128)(2,1)S(1)}, bf16[256,1024]{1,0:T(8,128)(2,1)S(1)}, u32[]{:S(2)}, u32[]{:S(2)}) collective-permute-start(bf16[256,1024]{1,0:T(8,128)(2,1)S(1)} %get-tuple-element.82.refs_0_), channel_id=1, source_target_pairs={{0,2},{1,3},{2,0},{3,1},{4,6},{5,7},{6,4},{7,5},{8,10},{9,11},{10,... | collective-permute-start | bytes 1572872 | tf_op jit(solution)/shard_map/ppermute | solution.py:237
  30.1 4.3 %constant_dynamic-slice_fusion = (bf16[1,1,2,512,256]{4,3,2,1,0:T(8,128)(2,1)}, bf16[1,1,2,512,256]{4,3,2,1,0:T(8,128)(2,1)}, bf16[1,1,2,512,256]{4,3,2,1,0:T(8,...) fusion(bf16[1,16,2,512,256]{4,3,2,1,0:T(8,128)(2,1)} %own.15, ...), kind=kLoop, calls=%fused_computation.55 | loop fusion | bytes 8388640 | tf_op jit(solution)/shard_map/dynamic_slice | solution.py:227
  34.5 1.8 collective-permute-start.5
  41.4 1.9 collective-permute-start.3
  43.3 1.5 collective-permute-start.4
  65.9 1.5 collective-permute-start.13
  67.4 2.2 project.5.queries.refs_5_
  72.0 6.0 %attend.8.refs_0_ = bf16[1024,256]{1,0:T(8,128)(2,1)S(1)} custom-call(s32[4]{0:T(128)S(1)} %pad_add_fusion.pick, bf16[1024,256]{1,0:T(8,128)(2,1)S(1)} %project.4.queries.refs_5_, bf16[1,16,2,512,256]{4,3,2,1,0:T(8,128)(2,1)} %own.15, bf16[1,1,2,512,256]{4,3,2,1,0:T(8,128)(2,1)S(1)} %copy-done.14, f32[2,33,128]{2,1,0:T(8,128)S(1)} %concatenate.9.table), custom_call_target="tpu_custom_call" | custom-call | flops 1073741824 | bytes 2097152 | tf_op jit(solution)/shard_map/attend/pallas_call | solution.py:73
  78.1 2.3 broadcast_select_fusion.10
  80.4 3.5 %collective-permute-start.10 = (bf16[1024,256]{1,0:T(8,128)(2,1)}, bf16[1024,256]{1,0:T(8,128)(2,1)}, u32[]{:S(2)}, u32[]{:S(2)}) collective-permute-start(bf16[1024,256]{1,0:T(8,128)(2,1)} %get-tuple-element.155), channel_id=1, source_target_pairs={{0,8},{4,12},{8,0},{12,4},{16,24},{20,28},{24,16},{28,20},{1,9},{5... | collective-permute-start | bytes 1572872 | tf_op jit(solution)/shard_map/ppermute | solution.py:291
  85.3 1.5 collective-permute-start.16
  92.2 6.0 %attend.9 = bf16[1024,256]{1,0:T(8,128)(2,1)S(1)} custom-call(s32[4]{0:T(128)S(1)} %pad_add_fusion.1.pick, bf16[1024,256]{1,0:T(8,128)(2,1)S(1)} %get-tuple-element.154.queries, bf16[1,16,2,512,256]{4,3,2,1,0:T(8,128)(2,1)} %own.15, bf16[1,1,2,512,256]{4,3,2,1,0:T(8,128)(2,1)S(1)} %collective-permute-done.12.other, f32[2,33,128]{2,1,0:T(8,128)S(1)} %concatenate.9.table), custom_call_target="tpu_custom_call" | custom-call | flops 1073741824 | bytes 2097152 | tf_op jit(solution)/shard_map/attend/pallas_call | solution.py:73
  98.3 2.1 broadcast_select_fusion.8
  100.4 3.5 %collective-permute-start.14 = (bf16[1024,256]{1,0:T(8,128)(2,1)}, bf16[1024,256]{1,0:T(8,128)(2,1)}, u32[]{:S(2)}, u32[]{:S(2)}) collective-permute-start(bf16[1024,256]{1,0:T(8,128)(2,1)} %get-tuple-element.153), channel_id=1, source_target_pairs={{0,8},{4,12},{8,0},{12,4},{16,24},{20,28},{24,16},{28,20},{1,9},{5... | collective-permute-start | bytes 1572872 | tf_op jit(solution)/shard_map/ppermute | solution.py:291
  103.9 1.5 collective-permute-start.15
  105.3 1.5 collective-permute-start.19
  111.4 1.5 collective-permute-start.18
  113.9 6.1 %attend.10 = bf16[1024,256]{1,0:T(8,128)(2,1)S(1)} custom-call(s32[4]{0:T(128)S(1)} %pad_add_fusion.2.pick, bf16[1024,256]{1,0:T(8,128)(2,1)S(1)} %get-tuple-element.152.queries, bf16[1,16,2,512,256]{4,3,2,1,0:T(8,128)(2,1)} %own.15, bf16[1,1,2,512,256]{4,3,2,1,0:T(8,128)(2,1)S(1)} %copy-done.12, f32[2,33,128]{2,1,0:T(8,128)S(1)} %concatenate.9.table), custom_call_target="tpu_custom_call" | custom-call | flops 1073741824 | bytes 2097152 | tf_op jit(solution)/shard_map/attend/pallas_call | solution.py:73
  120.9 4.0 %collective-permute-start.17 = (bf16[1024,256]{1,0:T(8,128)(2,1)}, bf16[1024,256]{1,0:T(8,128)(2,1)}, u32[]{:S(2)}, u32[]{:S(2)}) collective-permute-start(bf16[1024,256]{1,0:T(8,128)(2,1)} %broadcast_select_fusion.7), channel_id=1, source_target_pairs={{0,8},{4,12},{8,0},{12,4},{16,24},{20,28},{24,16},{28,20},{1,9},{5... | collective-permute-start | bytes 1572872 | tf_op jit(solution)/shard_map/ppermute | solution.py:291
  131.3 6.3 %attend.11 = bf16[1024,256]{1,0:T(8,128)(2,1)S(1)} custom-call(s32[4]{0:T(128)S(1)} %pad_add_fusion.3.pick, bf16[1024,256]{1,0:T(8,128)(2,1)S(1)} %broadcast_select_fusion.6.queries, bf16[1,16,2,512,256]{4,3,2,1,0:T(8,128)(2,1)} %own.15, bf16[1,1,2,512,256]{4,3,2,1,0:T(8,128)(2,1)} %collective-permute-done.13.other, f32[2,33,128]{2,1,0:T(8,128)S(1)} %concatenate.9.table), custom_call_target="tpu_custom_call" | custom-call | flops 1073741824 | bytes 2097152 | tf_op jit(solution)/shard_map/attend/pallas_call | solution.py:73
  137.6 2.1 broadcast_select_fusion.4
  139.7 1.5 collective-permute-start.21
  142.1 1.8 collective-permute-start.20
  143.8 1.5 collective-permute-start.25
  150.9 6.3 %attend.12 = bf16[1024,256]{1,0:T(8,128)(2,1)S(1)} custom-call(s32[4]{0:T(128)S(1)} %pad_add_fusion.4.pick, bf16[1024,256]{1,0:T(8,128)(2,1)S(1)} %copy-done.1, bf16[1,16,2,512,256]{4,3,2,1,0:T(8,128)(2,1)} %own.15, bf16[1,1,2,512,256]{4,3,2,1,0:T(8,128)(2,1)} %collective-permute-done.16.other, f32[2,33,128]{2,1,0:T(8,128)S(1)} %concatenate.9.table), custom_call_target="tpu_custom_call" | custom-call | flops 1073741824 | bytes 2097152 | tf_op jit(solution)/shard_map/attend/pallas_call | solution.py:73
  157.2 2.1 broadcast_select_fusion.2
  159.3 1.6 collective-permute-start.24
  161.8 2.4 collective-permute-start.23
  170.2 6.3 %attend.13 = bf16[1024,256]{1,0:T(8,128)(2,1)S(1)} custom-call(s32[4]{0:T(128)S(1)} %pad_add_fusion.5.pick, bf16[1024,256]{1,0:T(8,128)(2,1)S(1)} %copy-done.2, bf16[1,16,2,512,256]{4,3,2,1,0:T(8,128)(2,1)} %own.15, bf16[1,1,2,512,256]{4,3,2,1,0:T(8,128)(2,1)} %collective-permute-done.19.other, f32[2,33,128]{2,1,0:T(8,128)S(1)} %concatenate.9.table), custom_call_target="tpu_custom_call" | custom-call | flops 1073741824 | bytes 2097152 | tf_op jit(solution)/shard_map/attend/pallas_call | solution.py:73
  176.5 2.3 broadcast_select_fusion.1
  178.7 1.5 collective-permute-start.27
  180.2 2.0 add_select_fusion.1
  182.2 2.2 collective-permute-start.26
  189.3 2.5 %copy.24 = bf16[256,2,1024]{2,0,1:T(8,128)(2,1)} copy(bf16[256,2,1024]{2,1,0:T(2,128)(2,1)} %param.9) | data formatting | bytes 2097152 | tf_op args[0]
  198.6 1.6 collective-permute-start.32
  200.2 6.2 %attend.14 = bf16[1024,256]{1,0:T(8,128)(2,1)S(1)} custom-call(s32[4]{0:T(128)S(1)} %pad_add_fusion.6.pick, bf16[1024,256]{1,0:T(8,128)(2,1)S(1)} %copy-done, bf16[1,16,2,512,256]{4,3,2,1,0:T(8,128)(2,1)} %own.15, bf16[1,1,2,512,256]{4,3,2,1,0:T(8,128)(2,1)} %collective-permute-done.22.other, f32[2,33,128]{2,1,0:T(8,128)S(1)} %concatenate.9.table), custom_call_target="tpu_custom_call" | custom-call | flops 1073741824 | bytes 2097152 | tf_op jit(solution)/shard_map/attend/pallas_call | solution.py:73
  209.6 1.9 collective-permute-start.34
  211.5 2.0 project.6
  213.5 3.4 %project.7 = (bf16[1024,256]{1,0:T(8,128)(2,1)S(1)}, bf16[1024,256]{1,0:T(8,128)(2,1)S(1)}, bf16[1024,256]{1,0:T(8,128)(2,1)S(1)}) custom-call(bf16[256,1024]{1,0:T(8,128)(2,1)S(1)} %copy-done.4, bf16[256,1024]{1,0:T(8,128)(2,1)} %collective-permute-done.7.refs_1_, bf16[256,1024]{1,0:T(8,128)(2,1)} %collective-permute-done.8.refs_2_, ...), custom_call_target="tpu_custom_call" | custom-call | flops 1610612736 | bytes 3670016 | tf_op jit(solution)/shard_map/project/pallas_call | solution.py:120
  216.9 2.8 %finish.2 = bf16[1024,256]{1,0:T(8,128)(2,1)S(1)} custom-call(f32[2]{0:T(128)S(1)} %get-tuple-element.119.first_bias, bf16[1024,256]{1,0:T(8,128)(2,1)S(1)} %attend.8.refs_0_, bf16[1024,256]{1,0:T(8,128)(2,1)S(1)} %get-tuple-element.140.refs_1_, bf16[1024,256]{1,0:T(8,128)(2,1)} %collective-permute-done.21.refs_2_, ...), custom_call_target="tpu_custom_call" | custom-call | tf_op jit(solution)/shard_map/finish/pallas_call | solution.py:159
  220.2 6.2 %attend.15.refs_0_ = bf16[1024,256]{1,0:T(8,128)(2,1)S(1)} custom-call(s32[4]{0:T(128)S(1)} %pad_add_fusion.7.pick, bf16[1024,256]{1,0:T(8,128)(2,1)S(1)} %project.5.queries.refs_5_, bf16[1,16,2,512,256]{4,3,2,1,0:T(8,128)(2,1)} %own.15, bf16[1,1,2,512,256]{4,3,2,1,0:T(8,128)(2,1)} %collective-permute-done.25.other, f32[2,33,128]{2,1,0:T(8,128)S(1)} %concatenate.9.table), custom_call_target="tpu_custom_call" | custom-call | flops 1073741824 | bytes 2097152 | tf_op jit(solution)/shard_map/attend/pallas_call | solution.py:73
  228.0 1.6 finish.3
  234.0 1.9 combine.2
  235.9 2.5 %collective-permute-done.37.refs_2_ = bf16[256,256]{1,0:T(8,128)(2,1)S(1)} collective-permute-done((bf16[256,256]{1,0:T(8,128)(2,1)S(1)}, bf16[256,256]{1,0:T(8,128)(2,1)S(1)}, u32[]{:S(2)}, u32[]{:S(2)}) %collective-permute-start.37) | collective-permute-done | bytes 131104 | tf_op jit(solution)/shard_map/ppermute | solution.py:243
  241.7 1.8 combine.3
  243.7 2.0 copy.17
  (157 shorter events, 43.0 us)
Async XLA Ops:
  2.2 11.6 %copy-start.30 = (s32[16]{0:T(128)S(1)}, s32[16]{0:T(128)}, u32[]{:S(2)}) copy-start(s32[16]{0:T(128)} %param.14) | copy-start | bytes 196
  3.8 35.5 %copy-start.5 = (bf16[256,1024]{1,0:T(8,128)(2,1)}, bf16[256,1024]{1,0:T(8,128)(2,1)S(1)}, u32[]{:S(2)}) copy-start(bf16[256,1024]{1,0:T(8,128)(2,1)S(1)} %get-tuple-element.82.refs_0_) | copy-start | bytes 1572868
  3.8 63.6 %copy-start.3 = (bf16[256,1024]{1,0:T(8,128)(2,1)}, bf16[256,1024]{1,0:T(8,128)(2,1)S(1)}, u32[]{:S(2)}) copy-start(bf16[256,1024]{1,0:T(8,128)(2,1)S(1)} %get-tuple-element.94.refs_0_) | copy-start | bytes 1572868
  3.8 32.4 %collective-permute-start.1 = (bf16[256,1024]{1,0:T(8,128)(2,1)S(1)}, bf16[256,1024]{1,0:T(8,128)(2,1)S(1)}, u32[]{:S(2)}, u32[]{:S(2)}) collective-permute-start(bf16[256,1024]{1,0:T(8,128)(2,1)S(1)} %get-tuple-element.82.refs_0_), channel_id=1, source_target_pairs={{0,2},{1,3},{2,0},{3,1},{4,6},{5,7},{6,4},{7,5},{8,10},{9,11},{10,... | collective-permute-start | bytes 1572872 | tf_op jit(solution)/shard_map/ppermute | solution.py:237
  6.8 31.4 %collective-permute-start = (bf16[256,1024]{1,0:T(8,128)(2,1)S(1)}, bf16[256,1024]{1,0:T(8,128)(2,1)S(1)}, u32[]{:S(2)}, u32[]{:S(2)}) collective-permute-start(bf16[256,1024]{1,0:T(8,128)(2,1)S(1)} %get-tuple-element.82.refs_0_), channel_id=1, source_target_pairs={{0,1},{1,0},{2,3},{3,2},{4,5},{5,4},{6,7},{7,6},{8,9},{9,8},{10,11... | collective-permute-start | bytes 1572872 | tf_op jit(solution)/shard_map/ppermute | solution.py:238
  6.8 31.1 %collective-permute-start.8 = (bf16[256,1024]{1,0:T(8,128)(2,1)S(1)}, bf16[256,1024]{1,0:T(8,128)(2,1)}, u32[]{:S(2)}, u32[]{:S(2)}) collective-permute-start(bf16[256,1024]{1,0:T(8,128)(2,1)S(1)} %get-tuple-element.94.refs_0_), channel_id=1, source_target_pairs={{0,2},{1,3},{2,0},{3,1},{4,6},{5,7},{6,4},{7,5},{8,10},{9,11},{10,... | collective-permute-start | bytes 1572872 | tf_op jit(solution)/shard_map/ppermute | solution.py:237
  7.0 36.3 %collective-permute-start.7 = (bf16[256,1024]{1,0:T(8,128)(2,1)S(1)}, bf16[256,1024]{1,0:T(8,128)(2,1)}, u32[]{:S(2)}, u32[]{:S(2)}) collective-permute-start(bf16[256,1024]{1,0:T(8,128)(2,1)S(1)} %get-tuple-element.94.refs_0_), channel_id=1, source_target_pairs={{0,1},{1,0},{2,3},{3,2},{4,5},{5,4},{6,7},{7,6},{8,9},{9,8},{10,11... | collective-permute-start | bytes 1572872 | tf_op jit(solution)/shard_map/ppermute | solution.py:238
  34.5 35.2 %collective-permute-start.5 = (bf16[1,1,2,512,256]{4,3,2,1,0:T(8,128)(2,1)}, bf16[1,1,2,512,256]{4,3,2,1,0:T(8,128)(2,1)S(1)}, u32[]{:S(2)}, u32[]{:S(2)}) collective-permute-start(bf16[1,1,2,512,256]{4,3,2,1,0:T(8,128)(2,1)} %get-tuple-element.128), channel_id=1, source_target_pairs={{0,4},{4,0},{8,12},{12,8},{16,20},{20,16},{24,28},{28,24},{1,5},{5... | collective-permute-start | bytes 1572872 | tf_op jit(solution)/shard_map/ppermute | solution.py:278
  36.2 3.1 %collective-permute-start.2 = (bf16[256,1024]{1,0:T(8,128)(2,1)S(1)}, bf16[256,1024]{1,0:T(8,128)(2,1)S(1)}, u32[]{:S(2)}, u32[]{:S(2)}) collective-permute-start(bf16[256,1024]{1,0:T(8,128)(2,1)S(1)} %collective-permute-done.1.refs_2_), channel_id=1, source_target_pairs={{0,1},{1,0},{2,3},{3,2},{4,5},{5,4},{6,7},{7,6},{8,9},{9,8},{10,11... | collective-permute-start | bytes 1572872 | tf_op jit(solution)/shard_map/ppermute | solution.py:239
  38.0 22.6 %copy-start.31 = (s32[16]{0:T(128)S(1)}, s32[16]{0:T(128)}, u32[]{:S(2)}) copy-start(s32[16]{0:T(128)} %param.13) | copy-start | bytes 196
  38.0 27.9 %collective-permute-start.9 = (bf16[256,1024]{1,0:T(8,128)(2,1)}, bf16[256,1024]{1,0:T(8,128)(2,1)}, u32[]{:S(2)}, u32[]{:S(2)}) collective-permute-start(bf16[256,1024]{1,0:T(8,128)(2,1)} %collective-permute-done.8.refs_2_), channel_id=1, source_target_pairs={{0,1},{1,0},{2,3},{3,2},{4,5},{5,4},{6,7},{7,6},{8,9},{9,8},{10,11... | collective-permute-start | bytes 1572872 | tf_op jit(solution)/shard_map/ppermute | solution.py:239
  39.1 39.0 %collective-permute-start.6 = (bf16[1,1,2,512,256]{4,3,2,1,0:T(8,128)(2,1)}, bf16[1,1,2,512,256]{4,3,2,1,0:T(8,128)(2,1)S(1)}, u32[]{:S(2)}, u32[]{:S(2)}) collective-permute-start(bf16[1,1,2,512,256]{4,3,2,1,0:T(8,128)(2,1)} %get-tuple-element.127), channel_id=1, source_target_pairs={{0,4},{4,0},{8,12},{12,8},{16,20},{20,16},{24,28},{28,24},{1,5},{5... | collective-permute-start | bytes 1572872 | tf_op jit(solution)/shard_map/ppermute | solution.py:294
  41.4 36.6 %collective-permute-start.3 = (bf16[1024,256]{1,0:T(8,128)(2,1)S(1)}, bf16[1024,256]{1,0:T(8,128)(2,1)}, u32[]{:S(2)}, u32[]{:S(2)}) collective-permute-start(bf16[1024,256]{1,0:T(8,128)(2,1)S(1)} %project.4.queries.refs_5_), channel_id=1, source_target_pairs={{0,8},{4,12},{8,0},{12,4},{16,24},{20,28},{24,16},{28,20},{1,9},{5... | collective-permute-start | bytes 1572872 | tf_op jit(solution)/shard_map/ppermute | solution.py:291
  43.3 34.7 %collective-permute-start.4 = (bf16[1024,256]{1,0:T(8,128)(2,1)S(1)}, bf16[1024,256]{1,0:T(8,128)(2,1)}, u32[]{:S(2)}, u32[]{:S(2)}) collective-permute-start(bf16[1024,256]{1,0:T(8,128)(2,1)S(1)} %project.4.queries.refs_5_), channel_id=1, source_target_pairs={{8,16},{16,8},{12,20},{20,12},{9,17},{17,9},{13,21},{21,13},{10,18... | collective-permute-start | bytes 1572872 | tf_op jit(solution)/shard_map/ppermute | solution.py:292
  65.9 32.3 %collective-permute-start.13 = (bf16[1,1,2,512,256]{4,3,2,1,0:T(8,128)(2,1)}, bf16[1,1,2,512,256]{4,3,2,1,0:T(8,128)(2,1)}, u32[]{:S(2)}, u32[]{:S(2)}) collective-permute-start(bf16[1,1,2,512,256]{4,3,2,1,0:T(8,128)(2,1)} %get-tuple-element.126), channel_id=1, source_target_pairs={{0,4},{4,0},{8,12},{12,8},{16,20},{20,16},{24,28},{28,24},{1,5},{5... | collective-permute-start | bytes 1572872 | tf_op jit(solution)/shard_map/ppermute | solution.py:294
  70.4 21.7 %collective-permute-start.12 = (bf16[1,1,2,512,256]{4,3,2,1,0:T(8,128)(2,1)}, bf16[1,1,2,512,256]{4,3,2,1,0:T(8,128)(2,1)S(1)}, u32[]{:S(2)}, u32[]{:S(2)}) collective-permute-start(bf16[1,1,2,512,256]{4,3,2,1,0:T(8,128)(2,1)} %get-tuple-element.58), channel_id=1, source_target_pairs={{0,4},{4,0},{8,12},{12,8},{16,20},{20,16},{24,28},{28,24},{1,5},{5... | collective-permute-start | bytes 1572872 | tf_op jit(solution)/shard_map/ppermute | solution.py:282
  78.1 14.1 %copy-start.11 = (bf16[1,1,2,512,256]{4,3,2,1,0:T(8,128)(2,1)}, bf16[1,1,2,512,256]{4,3,2,1,0:T(8,128)(2,1)S(1)}, u32[]{:S(2)}) copy-start(bf16[1,1,2,512,256]{4,3,2,1,0:T(8,128)(2,1)S(1)} %collective-permute-done.6.other) | copy-start | bytes 1572868
  80.4 17.9 %collective-permute-start.10 = (bf16[1024,256]{1,0:T(8,128)(2,1)}, bf16[1024,256]{1,0:T(8,128)(2,1)}, u32[]{:S(2)}, u32[]{:S(2)}) collective-permute-start(bf16[1024,256]{1,0:T(8,128)(2,1)} %get-tuple-element.155), channel_id=1, source_target_pairs={{0,8},{4,12},{8,0},{12,4},{16,24},{20,28},{24,16},{28,20},{1,9},{5... | collective-permute-start | bytes 1572872 | tf_op jit(solution)/shard_map/ppermute | solution.py:291
  83.8 14.4 %collective-permute-start.11 = (bf16[1024,256]{1,0:T(8,128)(2,1)}, bf16[1024,256]{1,0:T(8,128)(2,1)}, u32[]{:S(2)}, u32[]{:S(2)}) collective-permute-start(bf16[1024,256]{1,0:T(8,128)(2,1)} %collective-permute-done.3), channel_id=1, source_target_pairs={{8,16},{16,8},{12,20},{20,12},{9,17},{17,9},{13,21},{21,13},{10,18... | collective-permute-start | bytes 1572872 | tf_op jit(solution)/shard_map/ppermute | solution.py:292
  85.3 34.8 %collective-permute-start.16 = (bf16[1,1,2,512,256]{4,3,2,1,0:T(8,128)(2,1)}, bf16[1,1,2,512,256]{4,3,2,1,0:T(8,128)(2,1)}, u32[]{:S(2)}, u32[]{:S(2)}) collective-permute-start(bf16[1,1,2,512,256]{4,3,2,1,0:T(8,128)(2,1)} %get-tuple-element.125), channel_id=1, source_target_pairs={{0,4},{4,0},{8,12},{12,8},{16,20},{20,16},{24,28},{28,24},{1,5},{5... | collective-permute-start | bytes 1572872 | tf_op jit(solution)/shard_map/ppermute | solution.py:294
  100.4 19.7 %collective-permute-start.14 = (bf16[1024,256]{1,0:T(8,128)(2,1)}, bf16[1024,256]{1,0:T(8,128)(2,1)}, u32[]{:S(2)}, u32[]{:S(2)}) collective-permute-start(bf16[1024,256]{1,0:T(8,128)(2,1)} %get-tuple-element.153), channel_id=1, source_target_pairs={{0,8},{4,12},{8,0},{12,4},{16,24},{20,28},{24,16},{28,20},{1,9},{5... | collective-permute-start | bytes 1572872 | tf_op jit(solution)/shard_map/ppermute | solution.py:291
  103.9 16.2 %collective-permute-start.15 = (bf16[1024,256]{1,0:T(8,128)(2,1)}, bf16[1024,256]{1,0:T(8,128)(2,1)}, u32[]{:S(2)}, u32[]{:S(2)}) collective-permute-start(bf16[1024,256]{1,0:T(8,128)(2,1)} %collective-permute-done.10), channel_id=1, source_target_pairs={{8,16},{16,8},{12,20},{20,12},{9,17},{17,9},{13,21},{21,13},{10,18... | collective-permute-start | bytes 1572872 | tf_op jit(solution)/shard_map/ppermute | solution.py:292
  105.3 32.3 %collective-permute-start.19 = (bf16[1,1,2,512,256]{4,3,2,1,0:T(8,128)(2,1)}, bf16[1,1,2,512,256]{4,3,2,1,0:T(8,128)(2,1)}, u32[]{:S(2)}, u32[]{:S(2)}) collective-permute-start(bf16[1,1,2,512,256]{4,3,2,1,0:T(8,128)(2,1)} %get-tuple-element.124), channel_id=1, source_target_pairs={{0,4},{4,0},{8,12},{12,8},{16,20},{20,16},{24,28},{28,24},{1,5},{5... | collective-permute-start | bytes 1572872 | tf_op jit(solution)/shard_map/ppermute | solution.py:294
  111.4 26.2 %collective-permute-start.18 = (bf16[1024,256]{1,0:T(8,128)(2,1)S(1)}, bf16[1024,256]{1,0:T(8,128)(2,1)}, u32[]{:S(2)}, u32[]{:S(2)}) collective-permute-start(bf16[1024,256]{1,0:T(8,128)(2,1)S(1)} %project.5.queries.refs_5_), channel_id=1, source_target_pairs={{8,16},{16,8},{12,20},{20,12},{9,17},{17,9},{13,21},{21,13},{10,18... | collective-permute-start | bytes 1572872 | tf_op jit(solution)/shard_map/ppermute | solution.py:292
  120.9 16.7 %collective-permute-start.17 = (bf16[1024,256]{1,0:T(8,128)(2,1)}, bf16[1024,256]{1,0:T(8,128)(2,1)}, u32[]{:S(2)}, u32[]{:S(2)}) collective-permute-start(bf16[1024,256]{1,0:T(8,128)(2,1)} %broadcast_select_fusion.7), channel_id=1, source_target_pairs={{0,8},{4,12},{8,0},{12,4},{16,24},{20,28},{24,16},{28,20},{1,9},{5... | collective-permute-start | bytes 1572872 | tf_op jit(solution)/shard_map/ppermute | solution.py:291
  125.0 32.2 %collective-permute-start.22 = (bf16[1,1,2,512,256]{4,3,2,1,0:T(8,128)(2,1)}, bf16[1,1,2,512,256]{4,3,2,1,0:T(8,128)(2,1)}, u32[]{:S(2)}, u32[]{:S(2)}) collective-permute-start(bf16[1,1,2,512,256]{4,3,2,1,0:T(8,128)(2,1)} %get-tuple-element.123), channel_id=1, source_target_pairs={{0,4},{4,0},{8,12},{12,8},{16,20},{20,16},{24,28},{28,24},{1,5},{5... | collective-permute-start | bytes 1572872 | tf_op jit(solution)/shard_map/ppermute | solution.py:294
  139.7 17.4 %collective-permute-start.21 = (bf16[1024,256]{1,0:T(8,128)(2,1)}, bf16[1024,256]{1,0:T(8,128)(2,1)}, u32[]{:S(2)}, u32[]{:S(2)}) collective-permute-start(bf16[1024,256]{1,0:T(8,128)(2,1)} %get-tuple-element.151), channel_id=1, source_target_pairs={{8,16},{16,8},{12,20},{20,12},{9,17},{17,9},{13,21},{21,13},{10,18... | collective-permute-start | bytes 1572872 | tf_op jit(solution)/shard_map/ppermute | solution.py:292
  142.1 15.1 %collective-permute-start.20 = (bf16[1024,256]{1,0:T(8,128)(2,1)}, bf16[1024,256]{1,0:T(8,128)(2,1)}, u32[]{:S(2)}, u32[]{:S(2)}) collective-permute-start(bf16[1024,256]{1,0:T(8,128)(2,1)} %broadcast_select_fusion.5), channel_id=1, source_target_pairs={{0,8},{4,12},{8,0},{12,4},{16,24},{20,28},{24,16},{28,20},{1,9},{5... | collective-permute-start | bytes 1572872 | tf_op jit(solution)/shard_map/ppermute | solution.py:291
  143.8 32.6 %collective-permute-start.25 = (bf16[1,1,2,512,256]{4,3,2,1,0:T(8,128)(2,1)}, bf16[1,1,2,512,256]{4,3,2,1,0:T(8,128)(2,1)}, u32[]{:S(2)}, u32[]{:S(2)}) collective-permute-start(bf16[1,1,2,512,256]{4,3,2,1,0:T(8,128)(2,1)} %get-tuple-element.122), channel_id=1, source_target_pairs={{0,4},{4,0},{8,12},{12,8},{16,20},{20,16},{24,28},{28,24},{1,5},{5... | collective-permute-start | bytes 1572872 | tf_op jit(solution)/shard_map/ppermute | solution.py:294
  159.3 17.1 %collective-permute-start.24 = (bf16[1024,256]{1,0:T(8,128)(2,1)}, bf16[1024,256]{1,0:T(8,128)(2,1)}, u32[]{:S(2)}, u32[]{:S(2)}) collective-permute-start(bf16[1024,256]{1,0:T(8,128)(2,1)} %get-tuple-element.149), channel_id=1, source_target_pairs={{8,16},{16,8},{12,20},{20,12},{9,17},{17,9},{13,21},{21,13},{10,18... | collective-permute-start | bytes 1572872 | tf_op jit(solution)/shard_map/ppermute | solution.py:292
  161.8 14.7 %collective-permute-start.23 = (bf16[1024,256]{1,0:T(8,128)(2,1)}, bf16[1024,256]{1,0:T(8,128)(2,1)}, u32[]{:S(2)}, u32[]{:S(2)}) collective-permute-start(bf16[1024,256]{1,0:T(8,128)(2,1)} %broadcast_select_fusion.3), channel_id=1, source_target_pairs={{0,8},{4,12},{8,0},{12,4},{16,24},{20,28},{24,16},{28,20},{1,9},{5... | collective-permute-start | bytes 1572872 | tf_op jit(solution)/shard_map/ppermute | solution.py:291
  176.4 7.9 %copy-start.25 = (bf16[128,8,4,256]{3,1,2,0:T(8,128)(2,1)S(1)}, bf16[128,8,4,256]{3,1,2,0:T(8,128)(2,1)}, u32[]{:S(2)}) copy-start(bf16[128,8,4,256]{3,1,2,0:T(8,128)(2,1)} %copy-done.24) | copy-start | bytes 6291460
  178.7 27.7 %collective-permute-start.27 = (bf16[1024,256]{1,0:T(8,128)(2,1)}, bf16[1024,256]{1,0:T(8,128)(2,1)}, u32[]{:S(2)}, u32[]{:S(2)}) collective-permute-start(bf16[1024,256]{1,0:T(8,128)(2,1)} %get-tuple-element.147), channel_id=1, source_target_pairs={{8,16},{16,8},{12,20},{20,12},{9,17},{17,9},{13,21},{21,13},{10,18... | collective-permute-start | bytes 1572872 | tf_op jit(solution)/shard_map/ppermute | solution.py:292
  182.2 15.1 %copy-start.28 = (bf16[1024,256]{1,0:T(8,128)(2,1)S(1)}, bf16[1024,256]{1,0:T(8,128)(2,1)}, u32[]{:S(2)}) copy-start(bf16[1024,256]{1,0:T(8,128)(2,1)} %get-tuple-element.130) | copy-start | bytes 1572868
  182.2 24.3 %collective-permute-start.26 = (bf16[1024,256]{1,0:T(8,128)(2,1)}, bf16[1024,256]{1,0:T(8,128)(2,1)}, u32[]{:S(2)}, u32[]{:S(2)}) collective-permute-start(bf16[1024,256]{1,0:T(8,128)(2,1)} %add_select_fusion.1), channel_id=1, source_target_pairs={{0,8},{4,12},{8,0},{12,4},{16,24},{20,28},{24,16},{28,20},{1,9},{5... | collective-permute-start | bytes 1572872 | tf_op jit(solution)/shard_map/ppermute | solution.py:291
  191.8 8.4 %copy-start = (bf16[1024,256]{1,0:T(8,128)(2,1)S(1)}, bf16[1024,256]{1,0:T(8,128)(2,1)}, u32[]{:S(2)}) copy-start(bf16[1024,256]{1,0:T(8,128)(2,1)} %get-tuple-element.146.queries) | copy-start | bytes 1572868
  198.6 18.2 %collective-permute-start.32 = (bf16[256,1024]{1,0:T(8,128)(2,1)}, bf16[256,1024]{1,0:T(8,128)(2,1)S(1)}, u32[]{:S(2)}, u32[]{:S(2)}) collective-permute-start(bf16[256,1024]{1,0:T(8,128)(2,1)} %refs_4_.1), channel_id=1, source_target_pairs={{0,2},{1,3},{2,0},{3,1},{4,6},{5,7},{6,4},{7,5},{8,10},{9,11},{10,... | collective-permute-start | bytes 1572872 | tf_op jit(solution)/shard_map/ppermute | solution.py:302
  200.2 29.5 %collective-permute-start.31 = (bf16[256,1024]{1,0:T(8,128)(2,1)}, bf16[256,1024]{1,0:T(8,128)(2,1)S(1)}, u32[]{:S(2)}, u32[]{:S(2)}) collective-permute-start(bf16[256,1024]{1,0:T(8,128)(2,1)} %refs_4_.1), channel_id=1, source_target_pairs={{0,1},{1,0},{2,3},{3,2},{4,5},{5,4},{6,7},{7,6},{8,9},{9,8},{10,11... | collective-permute-start | bytes 1572872 | tf_op jit(solution)/shard_map/ppermute | solution.py:306
  207.7 18.7 %collective-permute-start.35 = (bf16[1024,256]{1,0:T(8,128)(2,1)S(1)}, bf16[1024,256]{1,0:T(8,128)(2,1)S(1)}, u32[]{:S(2)}, u32[]{:S(2)}) collective-permute-start(bf16[1024,256]{1,0:T(8,128)(2,1)S(1)} %get-tuple-element.141), channel_id=1, source_target_pairs={{8,16},{16,8},{12,20},{20,12},{9,17},{17,9},{13,21},{21,13},{10,18... | collective-permute-start | bytes 1572872 | tf_op jit(solution)/shard_map/ppermute | solution.py:292
  209.6 17.5 %collective-permute-start.34 = (bf16[1024,256]{1,0:T(8,128)(2,1)S(1)}, bf16[1024,256]{1,0:T(8,128)(2,1)S(1)}, u32[]{:S(2)}, u32[]{:S(2)}) collective-permute-start(bf16[1024,256]{1,0:T(8,128)(2,1)S(1)} %add_select_fusion), channel_id=1, source_target_pairs={{0,8},{4,12},{8,0},{12,4},{16,24},{20,28},{24,16},{28,20},{1,9},{5... | collective-permute-start | bytes 1572872 | tf_op jit(solution)/shard_map/ppermute | solution.py:291
  216.8 17.2 %copy-start.7 = (bf16[256,1024]{1,0:T(8,128)(2,1)}, bf16[256,1024]{1,0:T(8,128)(2,1)S(1)}, u32[]{:S(2)}) copy-start(bf16[256,1024]{1,0:T(8,128)(2,1)S(1)} %collective-permute-done.32.refs_6_) | copy-start | bytes 1572868
  216.9 13.6 %collective-permute-start.33 = (bf16[256,1024]{1,0:T(8,128)(2,1)S(1)}, bf16[256,1024]{1,0:T(8,128)(2,1)S(1)}, u32[]{:S(2)}, u32[]{:S(2)}) collective-permute-start(bf16[256,1024]{1,0:T(8,128)(2,1)S(1)} %collective-permute-done.32.refs_6_), channel_id=1, source_target_pairs={{0,1},{1,0},{2,3},{3,2},{4,5},{5,4},{6,7},{7,6},{8,9},{9,8},{10,11... | collective-permute-start | bytes 1572872 | tf_op jit(solution)/shard_map/ppermute | solution.py:306
  219.8 11.2 %collective-permute-start.28 = (bf16[256,256]{1,0:T(8,128)(2,1)S(1)}, bf16[256,256]{1,0:T(8,128)(2,1)S(1)}, u32[]{:S(2)}, u32[]{:S(2)}) collective-permute-start(bf16[256,256]{1,0:T(8,128)(2,1)S(1)} %get-tuple-element.138), channel_id=1, source_target_pairs={{0,1},{1,0},{2,3},{3,2},{4,5},{5,4},{6,7},{7,6},{8,9},{9,8},{10,11... | collective-permute-start | bytes 393224 | tf_op jit(solution)/shard_map/ppermute | solution.py:243
  226.4 6.4 %collective-permute-start.29 = (bf16[256,256]{1,0:T(8,128)(2,1)S(1)}, bf16[256,256]{1,0:T(8,128)(2,1)S(1)}, u32[]{:S(2)}, u32[]{:S(2)}) collective-permute-start(bf16[256,256]{1,0:T(8,128)(2,1)S(1)} %get-tuple-element.137), channel_id=1, source_target_pairs={{0,2},{1,3},{2,0},{3,1},{4,6},{5,7},{6,4},{7,5},{8,10},{9,11},{10,... | collective-permute-start | bytes 393224 | tf_op jit(solution)/shard_map/ppermute | solution.py:243
  227.0 7.0 %collective-permute-start.30 = (bf16[256,256]{1,0:T(8,128)(2,1)S(1)}, bf16[256,256]{1,0:T(8,128)(2,1)S(1)}, u32[]{:S(2)}, u32[]{:S(2)}) collective-permute-start(bf16[256,256]{1,0:T(8,128)(2,1)S(1)} %get-tuple-element.136), channel_id=1, source_target_pairs={{0,3},{1,2},{2,1},{3,0},{4,7},{5,6},{6,5},{7,4},{8,11},{9,10},{10,... | collective-permute-start | bytes 393224 | tf_op jit(solution)/shard_map/ppermute | solution.py:243
  229.7 6.3 %collective-permute-start.36 = (bf16[256,256]{1,0:T(8,128)(2,1)S(1)}, bf16[256,256]{1,0:T(8,128)(2,1)S(1)}, u32[]{:S(2)}, u32[]{:S(2)}) collective-permute-start(bf16[256,256]{1,0:T(8,128)(2,1)S(1)} %get-tuple-element.144), channel_id=1, source_target_pairs={{0,1},{1,0},{2,3},{3,2},{4,5},{5,4},{6,7},{7,6},{8,9},{9,8},{10,11... | collective-permute-start | bytes 393224 | tf_op jit(solution)/shard_map/ppermute | solution.py:243
  230.4 8.0 %collective-permute-start.37 = (bf16[256,256]{1,0:T(8,128)(2,1)S(1)}, bf16[256,256]{1,0:T(8,128)(2,1)S(1)}, u32[]{:S(2)}, u32[]{:S(2)}) collective-permute-start(bf16[256,256]{1,0:T(8,128)(2,1)S(1)} %get-tuple-element.143), channel_id=1, source_target_pairs={{0,2},{1,3},{2,0},{3,1},{4,6},{5,7},{6,4},{7,5},{8,10},{9,11},{10,... | collective-permute-start | bytes 393224 | tf_op jit(solution)/shard_map/ppermute | solution.py:243
  231.0 8.7 %collective-permute-start.38 = (bf16[256,256]{1,0:T(8,128)(2,1)S(1)}, bf16[256,256]{1,0:T(8,128)(2,1)S(1)}, u32[]{:S(2)}, u32[]{:S(2)}) collective-permute-start(bf16[256,256]{1,0:T(8,128)(2,1)S(1)} %get-tuple-element.142), channel_id=1, source_target_pairs={{0,3},{1,2},{2,1},{3,0},{4,7},{5,6},{6,5},{7,4},{8,11},{9,10},{10,... | collective-permute-start | bytes 393224 | tf_op jit(solution)/shard_map/ppermute | solution.py:243
  (23 other events, 72.0 us)
